TPU v7x, 256 devices: a whole 4x4x8 slice. The times are simulated.
256 devices in a mesh: lon: 16 (over z, y_hi), lat: 8 (over x, y_lo), lev: 2 (over core).
Axes of the slice: x: 4, y: 4 (y_hi: 2, y_lo: 2; y = y_hi * 2 + y_lo), z: 8, core: 2. Of those that a mesh axis runs over, the one named last changes fastest.
Arguments:
- tokens: bfloat16 [8, 16, 256, 512], P('lev', 'lat', 'lon'), may hold values from -6 to 6
- w_qkv: bfloat16 [512, 1536], replicated
- w_out: bfloat16 [512, 512], replicated, may hold values from -0.25 to 0.25
- w_up: bfloat16 [512, 2048], replicated, may hold values from -0.25 to 0.25
- w_down: bfloat16 [2048, 512], replicated, may hold values from -0.125 to 0.125
- tile_mask: int32 [8, 16, 5], P('lat', 'lon'), may hold values 0 or 1
- level_group: int32 [8], replicated, may hold values from 0 to 1
- row_shift: int32 [16], P('lat'), may hold values from -24 to 24, as said below
Outputs:
- updated: bfloat16 [8, 16, 256, 512], P('lev', 'lat', 'lon')
Inputs may be any that keep to these rules, and one draw needn't show every extreme that they name: `row_shift`: each of the two extremes is taken by some row.
All inputs are finite; a program needn't handle non-finite values. No bound on the sum of `tile_mask` on one device may be relied on, other than what follows from the above.
Results may differ from a plain program's by a relative error of at most 0.0065.
Values may be sent and summed in bfloat16 or wider, within the bound.
A program may use at most 64 MiB of HBM per device.

v0:
```python
import jax
import jax.numpy as jnp
from jax import lax
from jax.sharding import PartitionSpec as P

HEADS = 16
HEAD_DIM = 32
OFFSETS = 5


def padded(array, sides, width):
    for axis, dim in sides:
        devices, length = (lax.axis_size(axis), array.shape[dim])
        up = [(i, (i + 1) % devices) for i in range(devices - 1)]
        down = [(j, i) for i, j in up]
        last = lax.slice_in_dim(array, length - width, length, axis=dim)
        initial = lax.slice_in_dim(array, 0, width, axis=dim)
        before = lax.ppermute(last, axis, up)
        after = lax.ppermute(initial, axis, down)
        array = jnp.concatenate([before, array, after], axis=dim)
    return array


def shifted(value, axis, steps):
    count = lax.axis_size(axis)
    pairs = [(source, (source + steps) % count) for source in range(count)]
    return lax.ppermute(value, axis, pairs)


def normalize(values):
    centred = values - jnp.mean(values, axis=-1, keepdims=True)
    spread = jnp.mean(centred * centred, axis=-1, keepdims=True)
    return centred * lax.rsqrt(spread + 1e-05)


def on_device(tokens, w_qkv, w_out, w_up, w_down, tile_mask, level_group, row_shift):
    own_levels, band_rows, tile_cols, width = tokens.shape
    query_rows = own_levels * band_rows * tile_cols
    inputs = tokens.astype(jnp.float32).reshape(query_rows, width)
    normed = normalize(inputs).astype(jnp.bfloat16)
    queries = (
        jnp.dot(normed, w_qkv[:, :width], preferred_element_type=jnp.float32) * HEAD_DIM ** (-0.5)
    ).astype(jnp.bfloat16)
    payload = jnp.dot(normed, w_qkv[:, width:], preferred_element_type=jnp.float32).astype(
        jnp.bfloat16
    )
    payload = payload.reshape(own_levels, band_rows, tile_cols, 2 * width)
    source = lax.all_gather(payload, "lev", axis=0, tiled=True)
    rimmed = padded(source, (("lat", 1),), 1)
    west_near = shifted(rimmed, "lon", 1)
    west_far = shifted(rimmed, "lon", 2)
    east_near = shifted(rimmed, "lon", -1)
    east_far = shifted(rimmed, "lon", -2)
    window = jnp.concatenate([west_far, west_near, rimmed, east_near, east_far], axis=2)
    key_count = window.shape[0] * window.shape[1] * window.shape[2]
    keyvals = window.reshape(key_count, 2 * width)
    band_index = lax.axis_index("lat")
    level_index = lax.axis_index("lev")
    lat_total = band_rows * lax.axis_size("lat")
    own_groups = lax.dynamic_slice_in_dim(level_group, level_index * own_levels, own_levels)
    same_group = own_groups[:, None] == level_group[None, :]
    query_row = band_index * band_rows + jnp.arange(band_rows)
    key_row = band_index * band_rows - 1 + jnp.arange(band_rows + 2)
    row_ok = (
        (jnp.abs(key_row[None, :] - query_row[:, None]) <= 1)
        & (key_row >= 0)[None, :]
        & (key_row < lat_total)[None, :]
    )
    offsets = jnp.arange(-2 * tile_cols, 3 * tile_cols)
    distance = offsets[None, :] - jnp.arange(tile_cols)[:, None]
    half = tile_cols // 2
    col_ok = (jnp.abs(distance) <= half)[None, :, :] | (
        jnp.abs(distance[None, :, :] - row_shift[:, None, None]) <= half
    )
    allowed = (tile_mask[0, 0] > 0) | (jnp.arange(OFFSETS) == OFFSETS // 2)
    tile_ok = jnp.repeat(allowed, tile_cols)
    visible = (
        same_group[:, None, None, :, None, None]
        & row_ok[None, :, None, None, :, None]
        & col_ok[None, :, :, None, None, :]
        & tile_ok
    )
    visible = visible.reshape(query_rows, key_count)
    span = 4 * HEAD_DIM
    pieces = []
    for group_start in range(0, HEADS, 4):
        lower = group_start * HEAD_DIM
        query_part = queries[:, lower : lower + span].reshape(query_rows, 4, HEAD_DIM)
        key_part = keyvals[:, lower : lower + span].reshape(key_count, 4, HEAD_DIM)
        value_part = keyvals[:, width + lower : width + lower + span].reshape(
            key_count, 4, HEAD_DIM
        )
        scores = jnp.einsum(
            "qhd,khd->hqk", query_part, key_part, preferred_element_type=jnp.float32
        )
        scores = jnp.where(visible[None], scores, -jnp.inf)
        highest = jnp.max(scores, axis=-1, keepdims=True)
        weights = jnp.exp(scores - highest)
        total = jnp.sum(weights, axis=-1)
        probs = weights.astype(jnp.bfloat16)
        weighted = jnp.einsum("hqk,khd->qhd", probs, value_part, preferred_element_type=jnp.float32)
        pieces.append((weighted / jnp.transpose(total)[:, :, None]).reshape(query_rows, span))
    attended = jnp.concatenate(pieces, axis=1).astype(jnp.bfloat16)
    middle = inputs + jnp.dot(attended, w_out, preferred_element_type=jnp.float32)
    mid_normed = normalize(middle).astype(jnp.bfloat16)
    hidden = jax.nn.gelu(
        jnp.dot(mid_normed, w_up, preferred_element_type=jnp.float32), approximate=False
    ).astype(jnp.bfloat16)
    updated = middle + jnp.dot(hidden, w_down, preferred_element_type=jnp.float32)
    return updated.astype(jnp.bfloat16).reshape(own_levels, band_rows, tile_cols, width)


def solution(mesh):
    placed = (
        P("lev", "lat", "lon", None),
        P(),
        P(),
        P(),
        P(),
        P("lat", "lon", None),
        P(),
        P("lat"),
    )
    return jax.shard_map(
        on_device,
        mesh=mesh,
        in_specs=placed,
        out_specs=P("lev", "lat", "lon", None),
        check_vma=False,
    )
```

profile of v0, /device:TPU:5, one launch (start us, length us, event | category | flops | bytes accessed | tf_op | source)
XLA Modules:
  0.0 122.6 jit_solution(14446960484812100078)
XLA Ops:
  0.0 1.2 convert_reduce_fusion
  1.2 1.1 multiply_reduce_fusion.1
  2.3 0.1 div.47
  2.4 0.1 rsqrt.20
  2.4 1.0 fusion.102
  3.5 1.6 %convolution_convert_fusion = bf16[128,1024]{1,0:T(8,128)(2,1)S(1)} fusion(bf16[128,512]{1,0:T(8,128)(2,1)S(1)} %fusion.102, bf16[512,1536]{1,0:T(8,128)(2,1)} %param.9), kind=kOutput, calls=%fused_computation.25 | convolution fusion | flops 134348800 | bytes 1441792 | tf_op jit(solution)/shard_map/dot_general | solution.py:44
  5.1 2.5 %all_gather.3 = bf16[8,2,16,1024]{3,2,1,0:T(8,128)(2,1)S(1)} all-gather(bf16[4,2,16,1024]{3,2,1,0:T(8,128)(2,1)S(1)} %bitcast.83), channel_id=1, replica_groups=mesh['lon'=16,'lat'=8,'lev'=2] {'lev'}, dimensions={0}, use_global_device_ids=true | all-gather | bytes 786432 | tf_op jit(solution)/shard_map/all_gather | solution.py:48
  7.6 0.8 fusion.148
  8.4 3.2 %collective-permute-start = (bf16[8,1,16,1024]{3,2,1,0:T(8,128)(2,1)}, bf16[8,1,16,1024]{3,2,1,0:T(8,128)(2,1)}, u32[]{:S(2)}, u32[]{:S(2)}) collective-permute-start(bf16[8,1,16,1024]{3,2,1,0:T(8,128)(2,1)} %get-tuple-element.14), channel_id=1, source_target_pairs={{0,2},{2,4},{4,6},{6,8},{8,10},{10,12},{12,14},{1,3},{3,5},{5,7},{... | collective-permute-start | bytes 786440 | tf_op jit(solution)/shard_map/ppermute | solution.py:18
  11.6 3.0 %collective-permute-start.1 = (bf16[8,1,16,1024]{3,2,1,0:T(8,128)(2,1)}, bf16[8,1,16,1024]{3,2,1,0:T(8,128)(2,1)S(1)}, u32[]{:S(2)}, u32[]{:S(2)}) collective-permute-start(bf16[8,1,16,1024]{3,2,1,0:T(8,128)(2,1)} %get-tuple-element.13), channel_id=1, source_target_pairs={{2,0},{4,2},{6,4},{8,6},{10,8},{12,10},{14,12},{3,1},{5,3},{7,5},{... | collective-permute-start | bytes 786440 | tf_op jit(solution)/shard_map/ppermute | solution.py:19
  14.7 0.7 dynamic_slice.3
  15.4 0.7 broadcast_compare_fusion
  16.2 0.1 broadcast_and_fusion.2
  16.3 0.7 fusion.115
  17.0 0.5 broadcast_and_fusion
  17.6 0.7 bitcast_or_fusion
  18.3 2.7 %and.92 = pred[128,2560]{1,0:T(8,128)(4,1)} reshape(pred[4,2,16,8,4,80]{5,4,3,2,1,0:T(4,128)(4,1)S(1)} %broadcast_and_fusion) | data formatting | bytes 655360 | tf_op jit(solution)/shard_map/and | solution.py:78
  21.1 0.1 and.93
  21.2 0.1 and.95
  21.3 1.6 %collective-permute-done = bf16[8,1,16,1024]{3,2,1,0:T(8,128)(2,1)} collective-permute-done((bf16[8,1,16,1024]{3,2,1,0:T(8,128)(2,1)}, bf16[8,1,16,1024]{3,2,1,0:T(8,128)(2,1)}, u32[]{:S(2)}, u32[]{:S(2)}) %collective-permute-start) | collective-permute-done | bytes 262176 | tf_op jit(solution)/shard_map/ppermute | solution.py:18
  22.8 1.7 %constant_dynamic-update-slice_fusion.2 = bf16[8,4,16,1024]{3,2,1,0:T(8,128)(2,1)} fusion(bf16[8,1,16,1024]{3,2,1,0:T(8,128)(2,1)} %collective-permute-done), kind=kLoop, calls=%fused_computation.114 | loop fusion | bytes 524288
  24.5 0.9 constant_dynamic-update-slice_fusion.1
  25.4 0.8 constant_dynamic-update-slice_fusion
  26.1 1.6 %collective-permute-start.2 = (bf16[8,4,16,1024]{3,2,1,0:T(8,128)(2,1)}, bf16[8,4,16,1024]{3,2,1,0:T(8,128)(2,1)}, u32[]{:S(2)}, u32[]{:S(2)}) collective-permute-start(bf16[8,4,16,1024]{3,2,1,0:T(8,128)(2,1)} %constant_dynamic-update-slice_fusion), channel_id=1, source_target_pairs={{0,32},{16,48},{32,64},{48,80},{64,96},{80,112},{96,128},{112,144}... | collective-permute-start | bytes 3145736 | tf_op jit(solution)/shard_map/ppermute | solution.py:27
  27.8 2.8 %collective-permute-start.3 = (bf16[8,4,16,1024]{3,2,1,0:T(8,128)(2,1)}, bf16[8,4,16,1024]{3,2,1,0:T(8,128)(2,1)}, u32[]{:S(2)}, u32[]{:S(2)}) collective-permute-start(bf16[8,4,16,1024]{3,2,1,0:T(8,128)(2,1)} %constant_dynamic-update-slice_fusion), channel_id=1, source_target_pairs={{0,16},{16,32},{32,48},{48,64},{64,80},{80,96},{96,112},{112,128},... | collective-permute-start | bytes 3145736 | tf_op jit(solution)/shard_map/ppermute | solution.py:27
  30.6 1.2 broadcast_and_fusion.1
  31.8 3.8 %collective-permute-start.4 = (bf16[8,4,16,1024]{3,2,1,0:T(8,128)(2,1)}, bf16[8,4,16,1024]{3,2,1,0:T(8,128)(2,1)}, u32[]{:S(2)}, u32[]{:S(2)}) collective-permute-start(bf16[8,4,16,1024]{3,2,1,0:T(8,128)(2,1)} %constant_dynamic-update-slice_fusion), channel_id=1, source_target_pairs={{0,240},{16,0},{32,16},{48,32},{64,48},{80,64},{96,80},{112,96},{1... | collective-permute-start | bytes 3145736 | tf_op jit(solution)/shard_map/ppermute | solution.py:27
  35.5 1.5 %collective-permute-start.5 = (bf16[8,4,16,1024]{3,2,1,0:T(8,128)(2,1)}, bf16[8,4,16,1024]{3,2,1,0:T(8,128)(2,1)}, u32[]{:S(2)}, u32[]{:S(2)}) collective-permute-start(bf16[8,4,16,1024]{3,2,1,0:T(8,128)(2,1)} %constant_dynamic-update-slice_fusion), channel_id=1, source_target_pairs={{0,224},{16,240},{32,0},{48,16},{64,32},{80,48},{96,64},{112,80},{... | collective-permute-start | bytes 3145736 | tf_op jit(solution)/shard_map/ppermute | solution.py:27
  37.0 1.3 %fusion.20 = bf16[128,512]{1,0:T(8,128)(2,1)S(1)} fusion(bf16[128,512]{1,0:T(8,128)(2,1)} %copy-done.12, bf16[512,1536]{1,0:T(8,128)(2,1)} %param.9), kind=kOutput, calls=%fused_computation.29 | convolution fusion | flops 67239936 | bytes 786432 | tf_op jit(solution)/shard_map/dot_general | solution.py:42
  38.4 0.1 copy.34
  38.5 0.1 copy.37
  38.6 0.1 copy.40
  38.7 0.1 copy.43
  38.9 15.5 %collective-permute-done.2 = bf16[8,4,16,1024]{3,2,1,0:T(8,128)(2,1)} collective-permute-done((bf16[8,4,16,1024]{3,2,1,0:T(8,128)(2,1)}, bf16[8,4,16,1024]{3,2,1,0:T(8,128)(2,1)}, u32[]{:S(2)}, u32[]{:S(2)}) %collective-permute-start.2) | collective-permute-done | bytes 1048608 | tf_op jit(solution)/shard_map/ppermute | solution.py:27
  54.3 1.3 %constant_dynamic-update-slice_fusion.9 = bf16[8,4,80,1024]{3,2,1,0:T(8,128)(2,1)S(1)} fusion(bf16[8,4,16,1024]{3,2,1,0:T(8,128)(2,1)} %collective-permute-done.2), kind=kLoop, calls=%fused_computation.121 | loop fusion | bytes 2097152
  55.6 23.9 %collective-permute-done.3 = bf16[8,4,16,1024]{3,2,1,0:T(8,128)(2,1)} collective-permute-done((bf16[8,4,16,1024]{3,2,1,0:T(8,128)(2,1)}, bf16[8,4,16,1024]{3,2,1,0:T(8,128)(2,1)}, u32[]{:S(2)}, u32[]{:S(2)}) %collective-permute-start.3) | collective-permute-done | bytes 1048608 | tf_op jit(solution)/shard_map/ppermute | solution.py:27
  79.5 1.3 %constant_dynamic-update-slice_fusion.8 = bf16[8,4,80,1024]{3,2,1,0:T(8,128)(2,1)S(1)} fusion(bf16[8,4,80,1024]{3,2,1,0:T(8,128)(2,1)S(1)} %constant_dynamic-update-slice_fusion.9, bf16[8,4,16,1024]{3,2,1,0:T(8,128)(2,1)} %collective-permute-done.3), kind=kLoop, calls=%fused_computation.120 | loop fusion | bytes 2097152
  80.8 1.0 constant_dynamic-update-slice_fusion.7
  81.9 1.3 %constant_dynamic-update-slice_fusion.4 = bf16[8,4,80,1024]{3,2,1,0:T(8,128)(2,1)S(1)} fusion(bf16[8,4,80,1024]{3,2,1,0:T(8,128)(2,1)S(1)} %constant_dynamic-update-slice_fusion.5, bf16[8,4,16,1024]{3,2,1,0:T(8,128)(2,1)} %collective-permute-done.4), kind=kLoop, calls=%fused_computation.116 | loop fusion | bytes 2097152
  83.2 1.3 %constant_dynamic-update-slice_fusion.3 = bf16[8,4,80,1024]{3,2,1,0:T(8,128)(2,1)S(1)} fusion(bf16[8,4,80,1024]{3,2,1,0:T(8,128)(2,1)S(1)} %constant_dynamic-update-slice_fusion.4, bf16[8,4,16,1024]{3,2,1,0:T(8,128)(2,1)} %collective-permute-done.5), kind=kLoop, calls=%fused_computation.115 | loop fusion | bytes 2097152 | tf_op jit(solution)/shard_map/concatenate | solution.py:54
  84.5 2.6 %fusion.147 = (bf16[2560,128]{1,0:T(8,128)(2,1)}, bf16[2560,128]{1,0:T(8,128)(2,1)S(1)}, bf16[2560,128]{1,0:T(8,128)(2,1)}, bf16[2560,128]{1,0:T(8,128)(2,1)}, b...) fusion(bf16[2560,1024]{1,0:T(8,128)(2,1)S(1)} %bitcast.73), kind=kLoop, calls=%fused_computation.170 | loop fusion | bytes 10485760 | tf_op jit(solution)/shard_map/slice | solution.py:89
  87.1 2.2 %copy.46 = bf16[2560,128]{0,1:T(8,128)(2,1)} copy(bf16[2560,128]{1,0:T(8,128)(2,1)} %get-tuple-element.5) | data formatting | bytes 1310720
  89.2 2.2 %copy.45 = bf16[2560,128]{0,1:T(8,128)(2,1)} copy(bf16[2560,128]{1,0:T(8,128)(2,1)} %get-tuple-element.11) | data formatting | bytes 1310720
  91.4 2.2 %copy.48 = bf16[2560,128]{0,1:T(8,128)(2,1)} copy(bf16[2560,128]{1,0:T(8,128)(2,1)} %get-tuple-element.9) | data formatting | bytes 1310720
  93.6 2.2 %copy.47 = bf16[2560,128]{0,1:T(8,128)(2,1)} copy(bf16[2560,128]{1,0:T(8,128)(2,1)} %get-tuple-element.10) | data formatting | bytes 1310720
  95.8 2.2 %copy.50 = bf16[2560,128]{0,1:T(8,128)(2,1)} copy(bf16[2560,128]{1,0:T(8,128)(2,1)} %get-tuple-element.7) | data formatting | bytes 1310720
  97.9 2.2 %copy.49 = bf16[2560,128]{0,1:T(8,128)(2,1)} copy(bf16[2560,128]{1,0:T(8,128)(2,1)} %get-tuple-element.8) | data formatting | bytes 1310720
  100.1 2.2 %copy.52 = bf16[2560,128]{0,1:T(8,128)(2,1)} copy(bf16[2560,128]{1,0:T(8,128)(2,1)} %get-tuple-element.12) | data formatting | bytes 1310720
  102.3 1.1 copy.51
  103.4 2.2 %fusion.153 = (f32[4,128]{1,0:T(4,128)S(1)}, f32[4,128,2560]{2,1,0:T(8,128)S(1)}) fusion(bf16[128,4,32]{0,2,1:T(8,128)(2,1)S(1)} %bitcast.87, bf16[2560,4,32]{0,2,1:T(8,128)(2,1)} %bitcast.81, pred[128,2560]{1,0:T(8,128)(4,1)S(1)} %broadcast_and_fusion.1), kind=kOutput, calls=%fused_computation.176 | convolution fusion | flops 86507008 | bytes 6260736 | tf_op jit(solution)/shard_map/qhd,khd->hqk/dot_general | solution.py:93
  105.6 0.8 fusion
  106.5 1.1 fusion.55
  107.6 1.1 fusion.152
  108.6 0.8 fusion.2
  109.5 1.1 fusion.52
  110.6 1.1 fusion.151
  111.6 0.8 fusion.4
  112.5 1.1 fusion.49
  113.6 1.3 %fusion.150 = (f32[4,128]{1,0:T(4,128)S(1)}, f32[4,128,2560]{2,1,0:T(8,128)S(1)}) fusion(bf16[128,4,32]{0,2,1:T(8,128)(2,1)S(1)} %bitcast.84, bf16[2560,4,32]{0,2,1:T(8,128)(2,1)S(1)} %bitcast.78, pred[128,2560]{1,0:T(8,128)(4,1)S(1)} %broadcast_and_fusion.1), kind=kOutput, calls=%fused_computation.173 | convolution fusion | flops 86507008 | bytes 6260736 | tf_op jit(solution)/shard_map/qhd,khd->hqk/dot_general | solution.py:93
  114.9 0.8 fusion.6
  115.7 1.1 fusion.46
  116.8 0.3 fusion.154
  117.2 0.2 multiply_reduce_fusion
  117.4 5.3 %fusion.21 = bf16[128,512]{1,0:T(8,128)(2,1)} fusion(f32[128,512]{1,0:T(8,128)S(1)} %get-tuple-element.28, bf16[2048,512]{1,0:T(8,128)(2,1)S(1)} %copy-done, bf16[512,2048]{1,0:T(8,128)(2,1)} %param.11, f32[128]{0:T(128)S(1)} %add_rsqrt_fusion.1, f32[128]{0:T(128)S(1)} %broadcast_multiply_fusion.1), kind=kOutput, calls=%fused_computation.30 | convolution fusion | flops 554237952 | bytes 4588544 | tf_op jit(solution)/shard_map/dot_general | solution.py:109
  (45 shorter events, 0.4 us)
Async XLA Ops:
  0.0 117.4 %copy-start = (bf16[2048,512]{1,0:T(8,128)(2,1)S(1)}, bf16[2048,512]{1,0:T(8,128)(2,1)}, u32[]{:S(2)}) copy-start(bf16[2048,512]{1,0:T(8,128)(2,1)} %param.12) | copy-start | bytes 6291460
  3.5 8.1 %copy-start.12 = (bf16[128,512]{1,0:T(8,128)(2,1)}, bf16[128,512]{1,0:T(8,128)(2,1)S(1)}, u32[]{:S(2)}) copy-start(bf16[128,512]{1,0:T(8,128)(2,1)S(1)} %fusion.102) | copy-start | bytes 393220
  8.4 14.4 %collective-permute-start = (bf16[8,1,16,1024]{3,2,1,0:T(8,128)(2,1)}, bf16[8,1,16,1024]{3,2,1,0:T(8,128)(2,1)}, u32[]{:S(2)}, u32[]{:S(2)}) collective-permute-start(bf16[8,1,16,1024]{3,2,1,0:T(8,128)(2,1)} %get-tuple-element.14), channel_id=1, source_target_pairs={{0,2},{2,4},{4,6},{6,8},{8,10},{10,12},{12,14},{1,3},{3,5},{5,7},{... | collective-permute-start | bytes 786440 | tf_op jit(solution)/shard_map/ppermute | solution.py:18
  11.6 13.7 %collective-permute-start.1 = (bf16[8,1,16,1024]{3,2,1,0:T(8,128)(2,1)}, bf16[8,1,16,1024]{3,2,1,0:T(8,128)(2,1)S(1)}, u32[]{:S(2)}, u32[]{:S(2)}) collective-permute-start(bf16[8,1,16,1024]{3,2,1,0:T(8,128)(2,1)} %get-tuple-element.13), channel_id=1, source_target_pairs={{2,0},{4,2},{6,4},{8,6},{10,8},{12,10},{14,12},{3,1},{5,3},{7,5},{... | collective-permute-start | bytes 786440 | tf_op jit(solution)/shard_map/ppermute | solution.py:19
  25.4 2.4 %copy-start.9 = (bf16[8,1,16,1024]{3,2,1,0:T(8,128)(2,1)}, bf16[8,1,16,1024]{3,2,1,0:T(8,128)(2,1)S(1)}, u32[]{:S(2)}) copy-start(bf16[8,1,16,1024]{3,2,1,0:T(8,128)(2,1)S(1)} %collective-permute-done.1) | copy-start | bytes 786436
  26.1 28.2 %collective-permute-start.2 = (bf16[8,4,16,1024]{3,2,1,0:T(8,128)(2,1)}, bf16[8,4,16,1024]{3,2,1,0:T(8,128)(2,1)}, u32[]{:S(2)}, u32[]{:S(2)}) collective-permute-start(bf16[8,4,16,1024]{3,2,1,0:T(8,128)(2,1)} %constant_dynamic-update-slice_fusion), channel_id=1, source_target_pairs={{0,32},{16,48},{32,64},{48,80},{64,96},{80,112},{96,128},{112,144}... | collective-permute-start | bytes 3145736 | tf_op jit(solution)/shard_map/ppermute | solution.py:27
  27.8 51.8 %collective-permute-start.3 = (bf16[8,4,16,1024]{3,2,1,0:T(8,128)(2,1)}, bf16[8,4,16,1024]{3,2,1,0:T(8,128)(2,1)}, u32[]{:S(2)}, u32[]{:S(2)}) collective-permute-start(bf16[8,4,16,1024]{3,2,1,0:T(8,128)(2,1)} %constant_dynamic-update-slice_fusion), channel_id=1, source_target_pairs={{0,16},{16,32},{32,48},{48,64},{64,80},{80,96},{96,112},{112,128},... | collective-permute-start | bytes 3145736 | tf_op jit(solution)/shard_map/ppermute | solution.py:27
  30.6 51.3 %copy-start.10 = (bf16[8,1,16,1024]{3,2,1,0:T(8,128)(2,1)S(1)}, bf16[8,1,16,1024]{3,2,1,0:T(8,128)(2,1)}, u32[]{:S(2)}) copy-start(bf16[8,1,16,1024]{3,2,1,0:T(8,128)(2,1)} %copy-done.9) | copy-start | bytes 786436
  31.8 50.1 %collective-permute-start.4 = (bf16[8,4,16,1024]{3,2,1,0:T(8,128)(2,1)}, bf16[8,4,16,1024]{3,2,1,0:T(8,128)(2,1)}, u32[]{:S(2)}, u32[]{:S(2)}) collective-permute-start(bf16[8,4,16,1024]{3,2,1,0:T(8,128)(2,1)} %constant_dynamic-update-slice_fusion), channel_id=1, source_target_pairs={{0,240},{16,0},{32,16},{48,32},{64,48},{80,64},{96,80},{112,96},{1... | collective-permute-start | bytes 3145736 | tf_op jit(solution)/shard_map/ppermute | solution.py:27
  35.5 47.7 %collective-permute-start.5 = (bf16[8,4,16,1024]{3,2,1,0:T(8,128)(2,1)}, bf16[8,4,16,1024]{3,2,1,0:T(8,128)(2,1)}, u32[]{:S(2)}, u32[]{:S(2)}) collective-permute-start(bf16[8,4,16,1024]{3,2,1,0:T(8,128)(2,1)} %constant_dynamic-update-slice_fusion), channel_id=1, source_target_pairs={{0,224},{16,240},{32,0},{48,16},{64,32},{80,48},{96,64},{112,80},{... | collective-permute-start | bytes 3145736 | tf_op jit(solution)/shard_map/ppermute | solution.py:27
  103.4 3.1 %copy-start.4 = (bf16[2560,128]{0,1:T(8,128)(2,1)S(1)}, bf16[2560,128]{0,1:T(8,128)(2,1)}, u32[]{:S(2)}) copy-start(bf16[2560,128]{0,1:T(8,128)(2,1)} %copy.45) | copy-start | bytes 1966084
  105.6 1.9 %copy-start.7 = (bf16[2560,128]{0,1:T(8,128)(2,1)S(1)}, bf16[2560,128]{0,1:T(8,128)(2,1)}, u32[]{:S(2)}) copy-start(bf16[2560,128]{0,1:T(8,128)(2,1)} %copy.48) | copy-start | bytes 1966084
  107.5 1.9 %copy-start.3 = (bf16[2560,128]{0,1:T(8,128)(2,1)S(1)}, bf16[2560,128]{0,1:T(8,128)(2,1)}, u32[]{:S(2)}) copy-start(bf16[2560,128]{0,1:T(8,128)(2,1)} %copy.47) | copy-start | bytes 1966084
  108.6 1.9 %copy-start.6 = (bf16[2560,128]{0,1:T(8,128)(2,1)S(1)}, bf16[2560,128]{0,1:T(8,128)(2,1)}, u32[]{:S(2)}) copy-start(bf16[2560,128]{0,1:T(8,128)(2,1)} %copy.50) | copy-start | bytes 1966084
  110.6 1.9 %copy-start.2 = (bf16[2560,128]{0,1:T(8,128)(2,1)S(1)}, bf16[2560,128]{0,1:T(8,128)(2,1)}, u32[]{:S(2)}) copy-start(bf16[2560,128]{0,1:T(8,128)(2,1)} %copy.49) | copy-start | bytes 1966084
  111.6 1.9 %copy-start.5 = (bf16[2560,128]{0,1:T(8,128)(2,1)S(1)}, bf16[2560,128]{0,1:T(8,128)(2,1)}, u32[]{:S(2)}) copy-start(bf16[2560,128]{0,1:T(8,128)(2,1)} %copy.52) | copy-start | bytes 1966084
  113.6 2.1 %copy-start.1 = (bf16[2560,128]{0,1:T(8,128)(2,1)S(1)}, bf16[2560,128]{0,1:T(8,128)(2,1)}, u32[]{:S(2)}) copy-start(bf16[2560,128]{0,1:T(8,128)(2,1)} %copy.51) | copy-start | bytes 1966084
  114.9 1.9 %copy-start.8 = (bf16[4,2,16,512]{3,2,1,0:T(8,128)(2,1)S(1)}, bf16[4,2,16,512]{3,2,1,0:T(8,128)(2,1)}, u32[]{:S(2)}) copy-start(bf16[4,2,16,512]{3,2,1,0:T(8,128)(2,1)} %param.8) | copy-start | bytes 393220
  114.9 2.0 %copy-start.11 = (bf16[512,512]{1,0:T(8,128)(2,1)S(1)}, bf16[512,512]{1,0:T(8,128)(2,1)}, u32[]{:S(2)}) copy-start(bf16[512,512]{1,0:T(8,128)(2,1)} %param.10) | copy-start | bytes 1572868
where the time goes:
time: 125 us; the launch traced here: 123 us
  waiting for transfers between devices  41 us (33%)
  local copies, waits for them, and re-layouts  33.7 us (27%)
  matrix products  18.4 us (15%)
  starting transfers between devices  15.8 us (13%)
  other arithmetic  10.9 us (9%)
  blocking collectives  2.49 us (2%)
    ppermute x4, waiting for transfers between devices, shifted(): return lax.ppermute(value, axis, pairs)  39.4 us
    unnamed x42, local copies, waits for them, and re-layouts  23.8 us
    ppermute x4, starting transfers between devices, shifted(): return lax.ppermute(value, axis, pairs)  9.64 us
    dot_general x4, matrix products, on_device(): jnp.einsum('qhd,khd->hqk', query_part, key_part, preferred_element_type=j...  5.59 us
    dot_general x1, matrix products, on_device(): jnp.dot(hidden, w_down, preferred_element_type=jnp.float32)  5.27 us
    dot_general x4, matrix products, on_device(): jnp.einsum('hqk,khd->qhd', probs, value_part, preferred_element_type=jnp....  4.3 us
    reduce_sum x4, other arithmetic, on_device(): total = jnp.sum(weights, axis=-1)  3.36 us
    ppermute x1, starting transfers between devices, padded(): before = lax.ppermute(last, axis, up)  3.19 us
  transfers between devices with their start and end apart: 6, of which 3 were waited for; matrix products, arithmetic and copies ran while one was open for 14% of the time, Pallas kernels for 0%

commit v1 on v0

v1 whole, which is shorter than its diff:
```python
import functools

import jax
import jax.numpy as jnp
from jax import lax
from jax.experimental import pallas as pl
from jax.experimental.pallas import tpu as pltpu
from jax.sharding import PartitionSpec as P

WIDTH = 512
HALF = 256
HEAD_DIM = 32
FF = 2048
EMPTY = -1e30
TINY = 1e-30
F32 = jnp.float32
BF16 = jnp.bfloat16
MESH = pl.DeviceIdType.MESH

M_PARTNER = 0
M_LOP = 2
M_XN = 3
M_PLOP = 4
M_PXN = 5
M_FAR = 6
M_OPP = 8
M_NEAR = 12
M_FAR_LOP = 14
M_FAR_XN = 15
M_OPP_PLOP = 16
M_OPP_PXN = 17
M_SIB = 18
M_PART = 20
M_WRAP = 22
M_OPP_LOP = 24
M_OPP_XN = 25
MESSAGES = 26


def normalize(values):
    centred = values - jnp.mean(values, axis=-1, keepdims=True)
    spread = jnp.mean(centred * centred, axis=-1, keepdims=True)
    return centred * lax.rsqrt(spread + 1e-05)


def kernel(
    tokens, w_qkv, w_out, w_up, w_down, tile_mask_h, level_group_h, row_shift_h, out,
    tile_mask, level_group, row_shift, win, sib, v_qkv, v_out, v_up, v_down, kv, queries, bias,
    bias_far, keep_o, keep_m,
    keep_l, part, got, send, recv, local, ready,
):
    lon, lat, lev = (lax.axis_index(a) for a in ("lon", "lat", "lev"))
    odd_lon, odd_lat = lax.rem(lon, 2), lax.rem(lat, 2)
    sigma, tau = 1 - 2 * odd_lon, 1 - 2 * odd_lat
    partner = lon + sigma
    lop = lat + tau
    xn = lax.rem(lat - tau + 8, 8)
    has_xn = (lat > 0) & (lat < 7)
    no_xn = (lat == 0) | (lat == 7)
    depth = lon // 2
    up, down = lax.rem(lon + 2, 16), lax.rem(lon + 14, 16)
    zp = lax.rem(lon + 2 * sigma + 16, 16)
    zm = lax.rem(lon - 2 * sigma + 16, 16)
    other = 1 - lev
    far, opp = 3 + odd_lon, 4 - odd_lon
    prow, xrow = 3 * (1 - odd_lat), 3 * odd_lat

    def device(lo=None, la=None, le=None):
        return (lon if lo is None else lo, lat if la is None else la, lev if le is None else le)

    last = depth == 7
    first = depth == 0
    wraps = lon == 15
    wrapped, wrapped_edges = lon == 0, lon == 1
    sends_near = (depth < 7) | (odd_lon == 1)
    sends_edges = (depth < 7) | (odd_lon == 0)
    takes_near = (depth > 0) | (odd_lon == 1)
    takes_edges = (depth > 0) | (odd_lon == 0)
    barrier = pltpu.get_barrier_semaphore()

    def greet(peer):
        pl.semaphore_signal(barrier, inc=1, device_id=peer, device_id_type=MESH)

    even_lon, even_lat = odd_lon == 0, odd_lat == 0
    beside = [
        (device(lo=partner), even_lon, None),
        (device(la=lop), even_lat, None),
        (device(la=xn), odd_lat == 1, has_xn),
        (device(lo=partner, la=lop), even_lon, None),
        (device(lo=partner, la=xn), even_lon, has_xn),
        (device(le=other), lev == 0, None),
    ]
    greetings = jnp.where(first, 0, 1) + jnp.where(last, 1, 0)
    for peer, greets, exists in beside:
        greetings += jnp.where(greets, 0, 1 if exists is None else jnp.where(exists, 1, 0))

        @pl.when(greets if exists is None else greets & exists)
        def _():
            greet(peer)

    @pl.when(depth < 7)
    def _():
        greet(device(lo=up))

    @pl.when(first)
    def _():
        greet(device(lo=down))

    @pl.when(wrapped)
    def _():
        greet(device(lo=15))

    loads = []
    for r in range(2):
        loads.append(pltpu.make_async_copy(tokens.at[:, r], win.at[0, 1 + r], local.at[r]))
    loads.append(pltpu.make_async_copy(w_qkv, v_qkv, local.at[2]))
    loads.append(pltpu.make_async_copy(w_out, v_out, local.at[3]))
    loads.append(pltpu.make_async_copy(w_up, v_up, local.at[4]))
    loads.append(pltpu.make_async_copy(w_down, v_down, local.at[5]))
    for load in loads:
        load.start()
    tables = [
        pltpu.make_async_copy(tile_mask_h, tile_mask, local.at[6]),
        pltpu.make_async_copy(level_group_h, level_group, local.at[7]),
        pltpu.make_async_copy(row_shift_h, row_shift, local.at[8]),
    ]
    for table in tables:
        table.start()

    greetings += jnp.where(wraps, 1, 0)
    @pl.when(greetings > 0)
    def _():
        pl.semaphore_wait(barrier, greetings)

    for number, (peer, greets, exists) in enumerate(beside):
        answers = jnp.logical_not(greets)

        @pl.when(answers if exists is None else answers & exists)
        def _():
            pl.semaphore_signal(ready.at[2 + number], inc=1, device_id=peer, device_id_type=MESH)

    def await_peer(*numbers):
        for number in numbers:
            _, greets, exists = beside[number]

            @pl.when(greets if exists is None else greets & exists)
            def _():
                pl.semaphore_wait(ready.at[2 + number], 1)

    @pl.when(depth > 0)
    def _():
        pl.semaphore_signal(ready.at[0], inc=1, device_id=device(lo=down), device_id_type=MESH)

    @pl.when(last)
    def _():
        pl.semaphore_signal(ready.at[1], inc=1, device_id=device(lo=up), device_id_type=MESH)

    up_row, down_row = 1 - odd_lat, odd_lat
    lop_at, xn_at = 3 * odd_lat, 3 * (1 - odd_lat)
    routes = {
        M_LOP: (tokens.at[:, up_row], win.at[0, lop_at], device(la=lop)),
        M_XN: (tokens.at[:, down_row], win.at[0, xn_at], device(la=xn)),
        M_PLOP: (tokens.at[:, up_row], win.at[1, lop_at], device(lo=partner, la=lop)),
        M_PXN: (tokens.at[:, down_row], win.at[1, xn_at], device(lo=partner, la=xn)),
        M_OPP + 2: (win.at[0, prow], win.at[opp, prow], device(lo=zm)),
        M_OPP + 3: (win.at[0, xrow], win.at[opp, xrow], device(lo=zm)),
        M_FAR_LOP: (win.at[far, 1 + up_row], win.at[far, lop_at], device(la=lop)),
        M_FAR_XN: (win.at[far, 1 + down_row], win.at[far, xn_at], device(la=xn)),
        M_OPP_LOP: (win.at[opp, 1 + up_row], win.at[opp, lop_at], device(la=lop)),
        M_OPP_XN: (win.at[opp, 1 + down_row], win.at[opp, xn_at], device(la=xn)),
        M_OPP_PLOP: (
            win.at[opp, 1 + up_row], win.at[2, lop_at], device(lo=partner, la=lop)),
        M_OPP_PXN: (
            win.at[opp, 1 + down_row], win.at[2, xn_at], device(lo=partner, la=xn)),
    }
    for r in range(2):
        routes[M_PARTNER + r] = (tokens.at[:, r], win.at[1, 1 + r], device(lo=partner))
        routes[M_FAR + r] = (tokens.at[:, r], win.at[far, 1 + r], device(lo=zp))
        routes[M_OPP + r] = (tokens.at[:, r], win.at[opp, 1 + r], device(lo=zm))
        routes[M_NEAR + r] = (win.at[1, 1 + r], win.at[2, 1 + r], device(lo=zp))
        routes[M_WRAP + r] = (tokens.at[:, r], win.at[2, 1 + r], device(lo=0))
        routes[M_SIB + r] = (tokens.at[:, r], sib.at[r], device(le=other))
        routes[M_PART + r] = (part.at[r], got.at[r], device(le=other))
    def message(number):
        src, dst, peer = routes[number]
        return pltpu.make_async_remote_copy(
            src_ref=src, dst_ref=dst, send_sem=send.at[number], recv_sem=recv.at[number],
            device_id=peer, device_id_type=MESH,
        )

    def begin(*numbers):
        for number in numbers:
            message(number).start()

    def arrived(*numbers):
        for number in numbers:
            message(number).wait_recv()

    zp_step = jnp.where(odd_lon == 0, jnp.where(last, 0, 1), jnp.where(first, 2, 0))
    zm_step = jnp.where(odd_lon == 1, jnp.where(last, 0, 1), jnp.where(first, 2, 0))

    def begin_z(step):
        @pl.when(zp_step == step)
        def _():
            begin(M_FAR, M_FAR + 1)

        @pl.when(zm_step == step)
        def _():
            begin(M_OPP, M_OPP + 1)

    begin_z(0)

    @pl.when(wraps)
    def _():
        begin(M_WRAP, M_WRAP + 1)

    await_peer(0)
    begin(M_PARTNER, M_PARTNER + 1)
    await_peer(5)
    begin(M_SIB, M_SIB + 1)

    @pl.when(depth < 7)
    def _():
        pl.semaphore_wait(ready.at[0], 1)

    begin_z(1)
    await_peer(1, 3, 2, 4)
    begin(M_LOP, M_PLOP)

    @pl.when(has_xn)
    def _():
        begin(M_XN, M_PXN)

    @pl.when(no_xn)
    def _():
        for slot in range(5):
            win[slot, xrow] = jnp.zeros((4, 16, WIDTH), BF16)

    def project_queries(owner, rows):
        normed = normalize(rows.astype(F32)).astype(BF16)
        q = jnp.dot(normed, v_qkv[:, :WIDTH], preferred_element_type=F32) * HEAD_DIM ** (-0.5)
        queries[owner] = q.astype(BF16).reshape(2, 64, WIDTH)

    def project_keys(places):
        rows = jnp.concatenate(
            [win[slot, row].reshape(64, WIDTH) for slot, row in places], axis=0)
        normed = normalize(rows.astype(F32)).astype(BF16)
        both = jnp.dot(normed, v_qkv[:, WIDTH:], preferred_element_type=F32).astype(BF16)
        for i, (slot, row) in enumerate(places):
            kv[slot, row] = both[64 * i:64 * (i + 1)]

    for load in loads[:3]:
        load.wait()
    project_queries(1, win[0, 1:3].reshape(128, WIDTH))

    project_keys([(0, 1), (0, 2)])

    for table in tables:
        table.wait()

    def iota(shape, dim):
        return lax.broadcasted_iota(jnp.int32, shape, dim)

    def spread(at, starts, values):
        result = jnp.full(at.shape, values[0], jnp.int32)
        for start, value in zip(starts[1:], values[1:]):
            result = jnp.where(at >= start, value, result)
        return result

    own_at = iota((64, 1), 0)
    q_col = own_at & 15
    q_lev = lax.shift_right_logical(own_at, 4)

    def pick(index, values):
        result = jnp.full(index.shape, values[0], jnp.int32)
        for i in range(1, len(values)):
            result = jnp.where(index == i, values[i], result)
        return result

    own_groups = [level_group[lev * 4 + i] for i in range(4)]
    q_groups = [
        pick(q_lev, [level_group[whose * 4 + i] for i in range(4)]) for whose in (other, lev)]
    dyn_slot = []
    for r in range(2):
        shift = row_shift[r]
        right = shift > 0
        dyn_slot.append(jnp.where(right, 4, 3))
        dyn_offset = jnp.where(right, 2, -2)
        dyn_ok = jnp.where(right, tile_mask[0, 0, 4], tile_mask[0, 0, 0])
        west, east = tile_mask[0, 0, 1], tile_mask[0, 0, 3]
        near_ok = jnp.where(odd_lon == 0, west, east)
        partner_ok = jnp.where(odd_lon == 0, east, west)
        edge = 3 * r
        for mask, starts, first_rows, offsets, tiles in (
            (bias, (0, 192, 384), (r, r, 1), (0, sigma, dyn_offset), (1, partner_ok, dyn_ok)),
            (bias_far, (0, 192), (r, edge), (-sigma, dyn_offset), (near_ok, dyn_ok)),
        ):
            at = iota((1, mask.shape[-1]), 1)
            in_segment = at - spread(at, starts, starts)
            key_row = lax.shift_right_logical(in_segment, 6) + spread(at, starts, first_rows)
            key_lev = lax.shift_right_logical(in_segment & 63, 4)
            key_col = in_segment & 15
            absolute = lat * 2 - 1 + key_row
            row_ok = (absolute >= 0) & (absolute < 16)
            offset = spread(at, starts, offsets)
            tile_ok = spread(at, starts, tiles)
            distance = offset * 16 + key_col - q_col
            near = (jnp.abs(distance) <= 8) | (jnp.abs(distance - shift) <= 8)
            near = near & (row_ok & (tile_ok > 0))
            key_group = pick(key_lev, own_groups)
            for owner in range(2):
                visible = near & (q_groups[owner] == key_group)
                mask[owner, r] = jnp.where(visible, 0.0, -jnp.inf).astype(F32)

    def forward_near(r):
        @pl.when(sends_near)
        def _():
            begin(M_NEAR + r)

    def forward_edges():
        @pl.when(sends_edges)
        def _():
            begin(M_OPP + 2)

            @pl.when(has_xn)
            def _():
                begin(M_OPP + 3)

    def forward_far():
        arrived(M_FAR, M_FAR + 1)
        begin(M_FAR_LOP)

        @pl.when(has_xn)
        def _():
            begin(M_FAR_XN)

    def forward_opp():
        arrived(M_OPP, M_OPP + 1)

        @pl.when(wrapped_edges)
        def _():
            begin(M_OPP_LOP)

            @pl.when(has_xn)
            def _():
                begin(M_OPP_XN)

        begin(M_OPP_PLOP)

        @pl.when(has_xn)
        def _():
            begin(M_OPP_PXN)

    def project_far():
        project_keys([(slot, row) for slot in (3, 4) for row in (1, 2)])

    arrived(M_PARTNER)

    @pl.when(first)
    def _():
        pl.semaphore_wait(ready.at[1], 1)

    begin_z(2)
    forward_near(0)
    arrived(M_PARTNER + 1)
    forward_near(1)
    arrived(M_LOP)

    @pl.when(has_xn)
    def _():
        arrived(M_XN)

    forward_edges()
    arrived(M_SIB, M_SIB + 1)
    project_queries(0, sib[...].reshape(128, WIDTH))

    pl.when(lon != 0)(forward_far)
    pl.when(lon != 1)(forward_opp)
    pl.when(depth > 0)(project_far)

    pl.when(lon == 0)(forward_far)
    pl.when(lon == 1)(forward_opp)
    arrived(M_PLOP)

    @pl.when(has_xn)
    def _():
        arrived(M_PXN)

    project_keys([(1, row) for row in range(4)] + [(0, 0), (0, 3)])


    pl.when(first)(project_far)

    lane_head = lax.shift_right_logical(iota((1, HALF), 1), 5)
    head_is = [lane_head == h for h in range(8)]
    head_one = [h.astype(F32).astype(BF16) for h in head_is]

    def attend(owner, r, half, phase, mask):
        lower = half * HALF
        q = queries[owner, r, :, lower:lower + HALF]
        stacked = jnp.concatenate([q * head_one[h] for h in range(8)], axis=0)
        pieces = [(dyn_slot[r], slice(1, 3) if phase == 0 else slice(3 * r, 3 * r + 1))]
        pieces = [(slot, slice(r, r + 3)) for slot in ((0, 1) if phase == 0 else (2,))] + pieces
        k, v = (
            jnp.concatenate([
                kv[slot, rows, :, start:start + HALF].reshape(-1, HALF) for slot, rows in pieces
            ], axis=0)
            for start in (lower, WIDTH + lower)
        )
        scores = lax.dot_general(
            stacked, k, (((1,), (1,)), ((), ())), preferred_element_type=F32)
        scores = scores.reshape(8, 64, -1) + mask[owner, r][None]
        highest = jnp.maximum(jnp.max(scores, axis=-1, keepdims=True), EMPTY)
        weights = jnp.exp(scores - highest)
        total = jnp.sum(weights, axis=-1, keepdims=True)
        probs = weights.astype(BF16).reshape(512, -1)
        summed = jnp.dot(probs, v, preferred_element_type=F32).reshape(8, 64, HALF)
        o, m, l = summed[0], highest[0], total[0]
        for h in range(1, 8):
            o = jnp.where(head_is[h], summed[h], o)
            m = jnp.where(head_is[h], highest[h], m)
            l = jnp.where(head_is[h], total[h], l)
        return o, m, l

    for owner in range(2):
        for r in range(2):
            for half in range(2):
                o, m, l = attend(owner, r, half, 0, bias)
                at = (owner, r, slice(None), slice(half * HALF, (half + 1) * HALF))
                keep_o[at], keep_m[at], keep_l[at] = o, m, l

    @pl.when(takes_near)
    def _():
        arrived(M_NEAR, M_NEAR + 1)

    @pl.when(wrapped)
    def _():
        arrived(M_WRAP, M_WRAP + 1)

    project_keys([(2, 1), (2, 2)])

    def merged(owner, r, half, phase, mask):
        o, m, l = attend(owner, r, half, phase, mask)
        at = (owner, r, slice(None), slice(half * HALF, (half + 1) * HALF))
        top = jnp.maximum(m, keep_m[at])
        old, new = jnp.exp(keep_m[at] - top), jnp.exp(m - top)
        return at, old * keep_o[at] + new * o, top, old * keep_l[at] + new * l

    @pl.when(takes_edges)
    def _():
        arrived(M_OPP + 2)

        @pl.when(has_xn)
        def _():
            arrived(M_OPP + 3)

    @pl.when(wrapped_edges)
    def _():
        arrived(M_OPP_LOP)

        @pl.when(has_xn)
        def _():
            arrived(M_OPP_XN)

    arrived(M_FAR_LOP, M_OPP_PLOP)

    @pl.when(has_xn)
    def _():
        arrived(M_FAR_XN, M_OPP_PXN)

    project_keys([(slot, row) for slot in (2, 3, 4) for row in (0, 3)])

    for owner in range(2):
        for r in range(2):
            for half in range(2):
                at, o, top, l = merged(owner, r, half, 1, bias_far)
                l = jnp.maximum(l, TINY)
                if owner == 0:
                    part[r, 0, :, at[-1]] = o / l
                    part[r, 1, :, at[-1]] = top + jnp.log(l)
                else:
                    keep_o[at], keep_m[at] = o / l, top + jnp.log(l)
            if owner == 0:
                begin(M_PART + r)

    rows = []
    for r in range(2):
        arrived(M_PART + r)
        mine, theirs = keep_m[1, r], got[r, 1]
        top = jnp.maximum(mine, theirs)
        mine, theirs = jnp.exp(mine - top), jnp.exp(theirs - top)
        rows.append((mine * keep_o[1, r] + theirs * got[r, 0]) / (mine + theirs))
    attended = jnp.concatenate(rows, axis=0).astype(BF16)

    for load in loads[3:]:
        load.wait()
    inputs = win[0, 1:3].reshape(128, WIDTH).astype(F32)
    middle = inputs + jnp.dot(attended, v_out[...], preferred_element_type=F32)
    mid_normed = normalize(middle).astype(BF16)
    updated = middle
    for start in range(0, FF, 512):
        hidden = jnp.dot(mid_normed, v_up[:, start:start + 512], preferred_element_type=F32)
        hidden = 0.5 * hidden * (1.0 + lax.erf(hidden * 0.5 ** 0.5))
        updated = updated + jnp.dot(
            hidden.astype(BF16), v_down[start:start + 512, :], preferred_element_type=F32)
    updated = updated.astype(BF16).reshape(2, 4, 16, WIDTH)
    for r in range(2):
        out[:, r] = updated[r]

    def sent(*numbers):
        for number in numbers:
            message(number).wait_send()

    sent(*range(M_PARTNER, M_PARTNER + 2), M_LOP, M_PLOP, M_FAR, M_FAR + 1, M_OPP, M_OPP + 1)
    sent(M_FAR_LOP, M_OPP_PLOP, M_SIB, M_SIB + 1, M_PART, M_PART + 1)

    @pl.when(has_xn)
    def _():
        sent(M_XN, M_PXN, M_FAR_XN, M_OPP_PXN)

    @pl.when(sends_near)
    def _():
        sent(M_NEAR, M_NEAR + 1)

    @pl.when(sends_edges)
    def _():
        sent(M_OPP + 2)

        @pl.when(has_xn)
        def _():
            sent(M_OPP + 3)

    @pl.when(wraps)
    def _():
        sent(M_WRAP, M_WRAP + 1)

    @pl.when(wrapped_edges)
    def _():
        sent(M_OPP_LOP)

        @pl.when(has_xn)
        def _():
            sent(M_OPP_XN)


def on_device(tokens, w_qkv, w_out, w_up, w_down, tile_mask, level_group, row_shift):
    anywhere = pl.BlockSpec(memory_space=pltpu.HBM)
    vmem = pltpu.VMEM
    return pl.pallas_call(
        kernel,
        out_shape=vmem(tokens.shape, BF16),
        in_specs=[anywhere] * 8,
        out_specs=pl.BlockSpec(memory_space=pltpu.VMEM),
        scratch_shapes=[
            pltpu.SMEM((1, 1, 5), jnp.int32),
            pltpu.SMEM((8,), jnp.int32),
            pltpu.SMEM((2,), jnp.int32),
            vmem((5, 4, 4, 16, WIDTH), BF16),
            vmem((2, 4, 16, WIDTH), BF16),
            vmem((WIDTH, 3 * WIDTH), BF16),
            vmem((WIDTH, WIDTH), BF16),
            vmem((WIDTH, FF), BF16),
            vmem((FF, WIDTH), BF16),
            vmem((5, 4, 64, 2 * WIDTH), BF16),
            vmem((2, 2, 64, WIDTH), BF16),
            vmem((2, 2, 64, 512), F32),
            vmem((2, 2, 64, 256), F32),
            vmem((2, 2, 64, WIDTH), F32),
            vmem((2, 2, 64, WIDTH), F32),
            vmem((2, 2, 64, WIDTH), F32),
            vmem((2, 2, 64, WIDTH), F32),
            vmem((2, 2, 64, WIDTH), F32),
            pltpu.SemaphoreType.DMA((MESSAGES,)),
            pltpu.SemaphoreType.DMA((MESSAGES,)),
            pltpu.SemaphoreType.DMA((9,)),
            pltpu.SemaphoreType.REGULAR((8,)),
        ],
        compiler_params=pltpu.CompilerParams(
            collective_id=0, has_side_effects=True, vmem_limit_bytes=60 * 1024 * 1024),
        cost_estimate=pl.CostEstimate(
            flops=6 * 10 ** 9, bytes_accessed=7 * 10 ** 6, transcendentals=4 * 10 ** 6),
    )(tokens, w_qkv, w_out, w_up, w_down, tile_mask, level_group, row_shift)


def solution(mesh):
    placed = (
        P("lev", "lat", "lon", None), P(), P(), P(), P(), P("lat", "lon", None), P(), P("lat"),
    )
    return jax.shard_map(
        on_device, mesh=mesh, in_specs=placed, out_specs=P("lev", "lat", "lon", None),
        check_vma=False,
    )
```

time: 125 us -> 25.9 us (0.21); the launches traced: 123 us -> 25.4 us
  waiting for transfers between devices: 41 us -> 0 us
  local copies, waits for them, and re-layouts: 33.7 us -> 0.66 us
  Pallas kernels: 0 us -> 24.8 us
  matrix products: 18.4 us -> 0 us
  starting transfers between devices: 15.8 us -> 0 us
  other arithmetic: 10.9 us -> 0 us
  blocking collectives: 2.49 us -> 0 us
    ppermute x6 -> x0, waiting for transfers between devices: 41 us -> none  [the longest x4 39.4 us: shifted(): return lax.ppermute(value, axis, pairs)]
    pallas_call x0 -> x1, Pallas kernels: none -> 24.8 us  [on_device(): pl.pallas_call(kernel, out_shape=vmem(tokens.shape, BF16), in_specs=[anyw...]
    unnamed x42 -> x1, local copies, waits for them, and re-layouts: 23.8 us -> 0.66 us
    dot_general x12 -> x0, matrix products: 18.4 us -> none  [the longest x4 5.59 us: on_device(): jnp.einsum('qhd,khd->hqk', query_part, key_part, preferred_element_type=j...]
    ppermute x6 -> x0, starting transfers between devices: 15.8 us -> none  [the longest x4 9.64 us: shifted(): return lax.ppermute(value, axis, pairs)]
    reduce_sum x7 -> x0, other arithmetic: 5.78 us -> none  [the longest x4 3.36 us: on_device(): total = jnp.sum(weights, axis=-1)]
    slice x7 -> x0, local copies, waits for them, and re-layouts: 3.89 us -> none  [the longest x1 2.55 us: on_device(): key_part = keyvals[:, lower:lower + span].reshape(key_count, 4, HEAD_DIM)]
    and x4 -> x0, local copies, waits for them, and re-layouts: 2.93 us -> none  [on_device(): same_group[:, None, None, :, None, None]]
  transfers between devices with their start and end apart: 6 -> 0, of which waited for: 3 -> 0; matrix products, arithmetic and copies ran while one was open for 14% -> 0% of each run, Pallas kernels for 0% -> 0%
where the time goes in v1:
time: 25.9 us; the launch traced here: 25.4 us
  Pallas kernels  24.8 us (96%)
  local copies, waits for them, and re-layouts  0.66 us (3%)
    pallas_call x1, Pallas kernels, on_device(): pl.pallas_call(kernel, out_shape=vmem(tokens.shape, BF16), in_specs=[anyw...  24.8 us
    unnamed x1, local copies, waits for them, and re-layouts  0.66 us

profile of v1, /device:TPU:5, one launch (start us, length us, event | category | flops | bytes accessed | tf_op | source)
XLA Modules:
  0.0 25.4 jit_solution(11160012105175233799)
XLA Ops:
  0.0 24.8 %shard_map.82 = bf16[4,2,16,512]{3,2,1,0:T(8,128)(2,1)S(1)} custom-call(bf16[4,2,16,512]{3,2,1,0:T(8,128)(2,1)} %tokens.1, bf16[512,1536]{1,0:T(8,128)(2,1)} %w_qkv.1, bf16[512,512]{1,0:T(8,128)(2,1)} %w_out.1, bf16[512,2048]{1,0:T(8,128)(2,1)} %w_up.1, bf16[2048,512]{1,0:T(8,128)(2,1)} %w_down.1, s32[1,1,5]{2,1,0:T(1,128)} %tile_mask_h.1, s32[8]{0:T(128)} %level_group_h.1, ...), custom_call_target="tpu_custom_call" | custom-call | flops 6000000000 | bytes 7000000 | tf_op jit(solution)/shard_map/pallas_call | solution.py:549
  24.8 0.7 %copy.10 = bf16[4,2,16,512]{3,2,1,0:T(8,128)(2,1)} copy(bf16[4,2,16,512]{3,2,1,0:T(8,128)(2,1)S(1)} %shard_map.82) | data formatting | bytes 262144

commit v2 on v1

--- a/solution.py
+++ b/solution.py
@@ -45,7 +45,7 @@
 
 def kernel(
     tokens, w_qkv, w_out, w_up, w_down, tile_mask_h, level_group_h, row_shift_h, out,
-    tile_mask, level_group, row_shift, win, sib, v_qkv, v_out, v_up, v_down, kv, queries, bias,
+    tile_mask, level_group, row_shift, win, sib, v_qkv, v_out, v_up, v_down, kv, kv_edge, queries, bias,
     bias_far, keep_o, keep_m,
     keep_l, part, got, send, recv, local, ready,
 ):
@@ -117,7 +117,7 @@
     loads.append(pltpu.make_async_copy(w_out, v_out, local.at[3]))
     loads.append(pltpu.make_async_copy(w_up, v_up, local.at[4]))
     loads.append(pltpu.make_async_copy(w_down, v_down, local.at[5]))
-    for load in loads:
+    for load in loads[:3]:
         load.start()
     tables = [
         pltpu.make_async_copy(tile_mask_h, tile_mask, local.at[6]),
@@ -210,12 +210,14 @@
 
     begin_z(0)
 
+    await_peer(0)
+    begin(M_PARTNER + 1)
+
     @pl.when(wraps)
     def _():
-        begin(M_WRAP, M_WRAP + 1)
-
-    await_peer(0)
-    begin(M_PARTNER, M_PARTNER + 1)
+        begin(M_WRAP)
+
+    begin(M_PARTNER)
     await_peer(5)
     begin(M_SIB, M_SIB + 1)
 
@@ -230,6 +232,9 @@
     @pl.when(has_xn)
     def _():
         begin(M_XN, M_PXN)
+
+    for load in loads[3:]:
+        load.start()
 
     @pl.when(no_xn)
     def _():
@@ -241,13 +246,15 @@
         q = jnp.dot(normed, v_qkv[:, :WIDTH], preferred_element_type=F32) * HEAD_DIM ** (-0.5)
         queries[owner] = q.astype(BF16).reshape(2, 64, WIDTH)
 
-    def project_keys(places):
-        rows = jnp.concatenate(
-            [win[slot, row].reshape(64, WIDTH) for slot, row in places], axis=0)
+    def project(pieces):
+        rows = jnp.concatenate([piece.reshape(64, WIDTH) for piece in pieces], axis=0)
         normed = normalize(rows.astype(F32)).astype(BF16)
         both = jnp.dot(normed, v_qkv[:, WIDTH:], preferred_element_type=F32).astype(BF16)
-        for i, (slot, row) in enumerate(places):
-            kv[slot, row] = both[64 * i:64 * (i + 1)]
+        return [both[64 * i:64 * (i + 1)] for i in range(len(pieces))]
+
+    def project_keys(places):
+        for (slot, row), piece in zip(places, project([win[place] for place in places])):
+            kv[slot, row] = piece
 
     for load in loads[:3]:
         load.wait()
@@ -313,9 +320,7 @@
                 mask[owner, r] = jnp.where(visible, 0.0, -jnp.inf).astype(F32)
 
     def forward_near(r):
-        @pl.when(sends_near)
-        def _():
-            begin(M_NEAR + r)
+        pl.when(sends_near | (r == 1))(lambda: begin(M_NEAR + r))
 
     def forward_edges():
         @pl.when(sends_edges)
@@ -354,16 +359,15 @@
     def project_far():
         project_keys([(slot, row) for slot in (3, 4) for row in (1, 2)])
 
-    arrived(M_PARTNER)
-
     @pl.when(first)
     def _():
         pl.semaphore_wait(ready.at[1], 1)
 
     begin_z(2)
-    forward_near(0)
     arrived(M_PARTNER + 1)
     forward_near(1)
+    arrived(M_PARTNER)
+    forward_near(0)
     arrived(M_LOP)
 
     @pl.when(has_xn)
@@ -399,14 +403,13 @@
         lower = half * HALF
         q = queries[owner, r, :, lower:lower + HALF]
         stacked = jnp.concatenate([q * head_one[h] for h in range(8)], axis=0)
-        pieces = [(dyn_slot[r], slice(1, 3) if phase == 0 else slice(3 * r, 3 * r + 1))]
-        pieces = [(slot, slice(r, r + 3)) for slot in ((0, 1) if phase == 0 else (2,))] + pieces
-        k, v = (
-            jnp.concatenate([
-                kv[slot, rows, :, start:start + HALF].reshape(-1, HALF) for slot, rows in pieces
-            ], axis=0)
-            for start in (lower, WIDTH + lower)
-        )
+        def gather(start):
+            lanes = slice(start, start + HALF)
+            pieces = [kv[slot, r:r + 3, :, lanes] for slot in ((0, 1) if phase == 0 else (2,))]
+            pieces.append(kv[dyn_slot[r], 1:3, :, lanes] if phase == 0 else kv_edge[r, :, lanes])
+            return jnp.concatenate([piece.reshape(-1, HALF) for piece in pieces], axis=0)
+
+        k, v = gather(lower), gather(WIDTH + lower)
         scores = lax.dot_general(
             stacked, k, (((1,), (1,)), ((), ())), preferred_element_type=F32)
         scores = scores.reshape(8, 64, -1) + mask[owner, r][None]
@@ -429,13 +432,15 @@
                 at = (owner, r, slice(None), slice(half * HALF, (half + 1) * HALF))
                 keep_o[at], keep_m[at], keep_l[at] = o, m, l
 
+    arrived(M_NEAR + 1)
+
     @pl.when(takes_near)
     def _():
-        arrived(M_NEAR, M_NEAR + 1)
+        arrived(M_NEAR)
 
     @pl.when(wrapped)
     def _():
-        arrived(M_WRAP, M_WRAP + 1)
+        arrived(M_WRAP)
 
     project_keys([(2, 1), (2, 2)])
 
@@ -468,7 +473,8 @@
     def _():
         arrived(M_FAR_XN, M_OPP_PXN)
 
-    project_keys([(slot, row) for slot in (2, 3, 4) for row in (0, 3)])
+    kv[2, 0], kv[2, 3], kv_edge[0], kv_edge[1] = project(
+        [win[2, 0], win[2, 3], win[dyn_slot[0], 0], win[dyn_slot[1], 3]])
 
     for owner in range(2):
         for r in range(2):
@@ -498,11 +504,11 @@
     middle = inputs + jnp.dot(attended, v_out[...], preferred_element_type=F32)
     mid_normed = normalize(middle).astype(BF16)
     updated = middle
-    for start in range(0, FF, 512):
-        hidden = jnp.dot(mid_normed, v_up[:, start:start + 512], preferred_element_type=F32)
+    for start in range(0, FF, 2048):
+        hidden = jnp.dot(mid_normed, v_up[:, start:start + 2048], preferred_element_type=F32)
         hidden = 0.5 * hidden * (1.0 + lax.erf(hidden * 0.5 ** 0.5))
         updated = updated + jnp.dot(
-            hidden.astype(BF16), v_down[start:start + 512, :], preferred_element_type=F32)
+            hidden.astype(BF16), v_down[start:start + 2048, :], preferred_element_type=F32)
     updated = updated.astype(BF16).reshape(2, 4, 16, WIDTH)
     for r in range(2):
         out[:, r] = updated[r]
@@ -520,7 +526,9 @@
 
     @pl.when(sends_near)
     def _():
-        sent(M_NEAR, M_NEAR + 1)
+        sent(M_NEAR)
+
+    sent(M_NEAR + 1)
 
     @pl.when(sends_edges)
     def _():
@@ -532,7 +540,7 @@
 
     @pl.when(wraps)
     def _():
-        sent(M_WRAP, M_WRAP + 1)
+        sent(M_WRAP)
 
     @pl.when(wrapped_edges)
     def _():
@@ -562,6 +570,7 @@
             vmem((WIDTH, FF), BF16),
             vmem((FF, WIDTH), BF16),
             vmem((5, 4, 64, 2 * WIDTH), BF16),
+            vmem((2, 64, 2 * WIDTH), BF16),
             vmem((2, 2, 64, WIDTH), BF16),
             vmem((2, 2, 64, 512), F32),
             vmem((2, 2, 64, 256), F32),

time: 25.9 us -> 23.9 us (0.923); the launches traced: 25.4 us -> 23.9 us
  Pallas kernels: 24.8 us -> 23.2 us
    pallas_call x1, Pallas kernels: 24.8 us -> 23.2 us  [on_device(): pl.pallas_call(kernel, out_shape=vmem(tokens.shape, BF16), in_specs=[anyw...]
where the time goes in v2:
time: 23.9 us
  Pallas kernels  23.2 us (97%)
  local copies, waits for them, and re-layouts  0.66 us (3%)
    pallas_call x1, Pallas kernels, on_device(): pl.pallas_call(kernel, out_shape=vmem(tokens.shape, BF16), in_specs=[anyw...  23.2 us
    unnamed x1, local copies, waits for them, and re-layouts  0.66 us

profile of v2, /device:TPU:5, one launch (start us, length us, event | category | flops | bytes accessed | tf_op | source)
XLA Modules:
  0.0 23.9 jit_solution(8975071351151154529)
XLA Ops:
  0.0 23.2 %shard_map.82 = bf16[4,2,16,512]{3,2,1,0:T(8,128)(2,1)S(1)} custom-call(bf16[4,2,16,512]{3,2,1,0:T(8,128)(2,1)} %tokens.1, bf16[512,1536]{1,0:T(8,128)(2,1)} %w_qkv.1, bf16[512,512]{1,0:T(8,128)(2,1)} %w_out.1, bf16[512,2048]{1,0:T(8,128)(2,1)} %w_up.1, bf16[2048,512]{1,0:T(8,128)(2,1)} %w_down.1, s32[1,1,5]{2,1,0:T(1,128)} %tile_mask_h.1, s32[8]{0:T(128)} %level_group_h.1, ...), custom_call_target="tpu_custom_call" | custom-call | flops 6000000000 | bytes 7000000 | tf_op jit(solution)/shard_map/pallas_call | solution.py:557
  23.2 0.7 %copy.10 = bf16[4,2,16,512]{3,2,1,0:T(8,128)(2,1)} copy(bf16[4,2,16,512]{3,2,1,0:T(8,128)(2,1)S(1)} %shard_map.82) | data formatting | bytes 262144

commit v3 on v2

--- a/solution.py
+++ b/solution.py
@@ -227,11 +227,12 @@
 
     begin_z(1)
     await_peer(1, 3, 2, 4)
+
+    @pl.when(has_xn)
+    def _():
+        begin(M_XN, M_PXN)
+
     begin(M_LOP, M_PLOP)
-
-    @pl.when(has_xn)
-    def _():
-        begin(M_XN, M_PXN)
 
     for load in loads[3:]:
         load.start()
@@ -333,28 +334,22 @@
 
     def forward_far():
         arrived(M_FAR, M_FAR + 1)
+        @pl.when(has_xn)
+        def _():
+            begin(M_FAR_XN)
+
         begin(M_FAR_LOP)
-
-        @pl.when(has_xn)
-        def _():
-            begin(M_FAR_XN)
 
     def forward_opp():
         arrived(M_OPP, M_OPP + 1)
 
-        @pl.when(wrapped_edges)
-        def _():
-            begin(M_OPP_LOP)
-
-            @pl.when(has_xn)
-            def _():
-                begin(M_OPP_XN)
-
+        @pl.when(has_xn)
+        def _():
+            pl.when(wrapped_edges)(lambda: begin(M_OPP_XN))
+            begin(M_OPP_PXN)
+
+        pl.when(wrapped_edges)(lambda: begin(M_OPP_LOP))
         begin(M_OPP_PLOP)
-
-        @pl.when(has_xn)
-        def _():
-            begin(M_OPP_PXN)
 
     def project_far():
         project_keys([(slot, row) for slot in (3, 4) for row in (1, 2)])

time: 23.9 us -> 23.9 us (level)
  no operation moved by 1% of the time
where the time goes in v3:
time: 23.9 us
  Pallas kernels  23.2 us (97%)
  local copies, waits for them, and re-layouts  0.66 us (3%)
    pallas_call x1, Pallas kernels, on_device(): pl.pallas_call(kernel, out_shape=vmem(tokens.shape, BF16), in_specs=[anyw...  23.2 us
    unnamed x1, local copies, waits for them, and re-layouts  0.66 us

profile of v3, /device:TPU:5, one launch (start us, length us, event | category | flops | bytes accessed | tf_op | source)
XLA Modules:
  0.0 23.9 jit_solution(11454625813563499690)
XLA Ops:
  0.0 23.2 %shard_map.82 = bf16[4,2,16,512]{3,2,1,0:T(8,128)(2,1)S(1)} custom-call(bf16[4,2,16,512]{3,2,1,0:T(8,128)(2,1)} %tokens.1, bf16[512,1536]{1,0:T(8,128)(2,1)} %w_qkv.1, bf16[512,512]{1,0:T(8,128)(2,1)} %w_out.1, bf16[512,2048]{1,0:T(8,128)(2,1)} %w_up.1, bf16[2048,512]{1,0:T(8,128)(2,1)} %w_down.1, s32[1,1,5]{2,1,0:T(1,128)} %tile_mask_h.1, s32[8]{0:T(128)} %level_group_h.1, ...), custom_call_target="tpu_custom_call" | custom-call | flops 6000000000 | bytes 7000000 | tf_op jit(solution)/shard_map/pallas_call | solution.py:552
  23.2 0.7 %copy.10 = bf16[4,2,16,512]{3,2,1,0:T(8,128)(2,1)} copy(bf16[4,2,16,512]{3,2,1,0:T(8,128)(2,1)S(1)} %shard_map.82) | data formatting | bytes 262144
